TPU v7x, 32 devices: a whole 2x2x4 slice. The times are simulated.
32 devices in a mesh: section: 2 (over core), dp: 16 (over z, y, x).
Axes of the slice: x: 2, y: 2, z: 4, core: 2. Of those that a mesh axis runs over, the one named last changes fastest.
Arguments:
- padded_segments: float32 [49152, 126], P('dp'), may hold values from -6 to 6
- history_extents: int32 [49152], P('dp'), may hold values from 36 to 126
- loss_prediction_adjoint: float32 [49152, 18], P('dp'), may hold values from -6 to 6
- first_layer: float32 [2, 126, 512], P('section', None, 'dp'), may hold values from -1 to 1
- square_layers: float32 [2, 5, 512, 512], P('section', None, 'dp'), may hold values from -0.25 to 0.25
- head_layer: float32 [2, 512, 144], P('section', 'dp'), may hold values from -0.25 to 0.25
- biases: float32 [2, 4, 512], P('section', None, 'dp'), may hold values from -0.875 to 0.875
- first_momentum: float32 [2, 126, 512], P('section', None, 'dp'), may hold values from -0.00036621094 to 0.00036621094
- square_momentum: float32 [2, 5, 512, 512], P('section', None, 'dp'), may hold values from -0.00036621094 to 0.00036621094
- head_momentum: float32 [2, 512, 144], P('section', 'dp'), may hold values from -0.00036621094 to 0.00036621094
- biases_momentum: float32 [2, 4, 512], P('section', None, 'dp'), may hold values from -0.00036621094 to 0.00036621094
- first_variance: float32 [2, 126, 512], P('section', None, 'dp'), may hold values from 3.4458802e-10 to 1.3783521e-09
- square_variance: float32 [2, 5, 512, 512], P('section', None, 'dp'), may hold values from 3.4458802e-10 to 1.3783521e-09
- head_variance: float32 [2, 512, 144], P('section', 'dp'), may hold values from 3.4458802e-10 to 1.3783521e-09
- biases_variance: float32 [2, 4, 512], P('section', None, 'dp'), may hold values from 3.4458802e-10 to 1.3783521e-09
Outputs:
- prediction_series: float32 [2, 49152, 18], P('section', 'dp')
- unit_entry_sensitivity: float32 [2, 49152, 126], P('section', 'dp')
- overall_slope_magnitude: float32 [], replicated
- first_grad: float32 [2, 126, 512], P('section', None, 'dp')
- square_grad: float32 [2, 5, 512, 512], P('section', None, 'dp')
- head_grad: float32 [2, 512, 144], P('section', 'dp')
- biases_grad: float32 [2, 4, 512], P('section', None, 'dp')
- first_layer_new: float32 [2, 126, 512], P('section', None, 'dp')
- square_layers_new: float32 [2, 5, 512, 512], P('section', None, 'dp')
- head_layer_new: float32 [2, 512, 144], P('section', 'dp')
- biases_new: float32 [2, 4, 512], P('section', None, 'dp')
- first_momentum_new: float32 [2, 126, 512], P('section', None, 'dp')
- square_momentum_new: float32 [2, 5, 512, 512], P('section', None, 'dp')
- head_momentum_new: float32 [2, 512, 144], P('section', 'dp')
- biases_momentum_new: float32 [2, 4, 512], P('section', None, 'dp')
- first_variance_new: float32 [2, 126, 512], P('section', None, 'dp')
- square_variance_new: float32 [2, 5, 512, 512], P('section', None, 'dp')
- head_variance_new: float32 [2, 512, 144], P('section', 'dp')
- biases_variance_new: float32 [2, 4, 512], P('section', None, 'dp')
Inputs may be any that keep to these rules, and one draw needn't show every extreme that they name: `history_extents`: a window's data are its last lengths positions, the earlier ones are padding.
All inputs are finite; a program needn't handle non-finite values.
Results may differ from a plain program's by a relative error of at most 0.013.
The roundings to bfloat16 on the way count: a program that leaves them out, or rounds other values in their place, can miss the bound.
Values may be sent and summed in bfloat16 or wider, within the bound.
A program may use at most 128 MiB of HBM per device.

v0:
```python
import functools

import jax
import jax.numpy as jnp
from jax import lax
from jax.experimental import pallas as pl
from jax.experimental.pallas import tpu as pltpu
from jax.sharding import PartitionSpec as P

STEP = 10


def dot_nn(a, b):
    return jnp.dot(a, b, preferred_element_type=jnp.float32)


def dot_tn(a, b):
    return lax.dot_general(a, b, (((0,), (0,)), ((), ())), preferred_element_type=jnp.float32)


def dot_nt(a, b):
    return lax.dot_general(a, b, (((1,), (1,)), ((), ())), preferred_element_type=jnp.float32)


def unit_rows(first, square, head, biases):
    units = first.shape[1]
    return jnp.concatenate(
        [square.transpose(1, 0, 2).reshape(units, -1), first.T, head, biases.T], axis=1
    )


def from_unit_rows(rows, past, hidden, out):
    wide = 5 * hidden
    square = rows[:, :wide].reshape(-1, 5, hidden).transpose(1, 0, 2)
    first = rows[:, wide : wide + past].T
    head = rows[:, wide + past : wide + past + out]
    biases = rows[:, wide + past + out :].T
    return first, square, head, biases


def plain_forward(weights, resid):
    first, square, head, biases = weights
    past = resid.shape[1]
    acts, slopes = [resid.astype(jnp.bfloat16)], []
    for k in range(4):
        z = dot_nn(acts[-1], first if k == 0 else square[k - 1]) + biases[k].astype(jnp.float32)
        sig = jax.nn.sigmoid(z)
        acts.append((z * sig).astype(jnp.bfloat16))
        slopes.append(sig * (1.0 + z * (1.0 - sig)))
    theta_b = dot_nn(acts[4], square[3]).astype(jnp.bfloat16)
    theta_f = dot_nn(acts[4], square[4]).astype(jnp.bfloat16)
    backcast = dot_nn(theta_b, head[:, :past])
    part = dot_nn(theta_f, head[:, past:])
    return backcast, part, (acts, slopes, theta_b, theta_f)


def plain_backward(weights, saved, e, f):
    first, square, head, biases = weights
    acts, slopes, theta_b, theta_f = saved
    past = e.shape[1]
    head_grad = jnp.concatenate([dot_tn(theta_b, e), dot_tn(theta_f, f)], axis=1)
    u_b = dot_nt(e, head[:, :past]).astype(jnp.bfloat16)
    u_f = dot_nt(f, head[:, past:]).astype(jnp.bfloat16)
    squares = [None, None, None, dot_tn(acts[4], u_b), dot_tn(acts[4], u_f)]
    da = dot_nt(u_b, square[3]) + dot_nt(u_f, square[4])
    bias_grads = [None] * 4
    first_grad = None
    for k in (3, 2, 1, 0):
        dz = (da * slopes[k]).astype(jnp.bfloat16)
        bias_grads[k] = jnp.sum(dz, axis=0, dtype=jnp.float32)
        grad = dot_tn(acts[k], dz)
        if k == 0:
            first_grad = grad
        else:
            squares[k - 1] = grad
        da = dot_nt(dz, first if k == 0 else square[k - 1])
    return da, (first_grad, jnp.stack(squares), head_grad, jnp.stack(bias_grads))


def adamw(master, gradient, momentum, variance, factor):
    clipped = gradient * factor
    moment_new = 0.9 * momentum + 0.1 * clipped
    variance_new = 0.999 * variance + 0.001 * clipped * clipped
    ratio = moment_new / (1.0 - 0.9**STEP) / (jnp.sqrt(variance_new / (1.0 - 0.999**STEP)) + 1e-08)
    return master - 0.05 * (ratio + 0.01 * master), moment_new, variance_new


def plain_shards(segments, extents, adjoint, *state):
    masters, momenta, variances = state[:4], state[4:8], state[8:]
    core = lax.axis_index("section")
    past, span = segments.shape[1], adjoint.shape[1]
    windows = segments.shape[0] // 2
    hidden = masters[1].shape[3]
    mine = [
        lax.dynamic_slice_in_dim(v, core * windows, windows, 0) for v in (segments, extents, adjoint)
    ]
    seg, ext, adj = mine
    rows = unit_rows(*(m[0].astype(jnp.bfloat16) for m in masters))
    rows = lax.all_gather(rows, "dp", axis=0, tiled=True)
    rows = lax.all_gather(rows, "section", axis=0)
    blocks = [from_unit_rows(rows[b], past, hidden, past + span) for b in range(2)]
    mask = (
        lax.broadcasted_iota(jnp.int32, (windows, past), 1) >= past - ext[:, None]
    ).astype(jnp.float32)
    r0 = seg * mask
    backcast, part0, saved0 = plain_forward(blocks[0], r0)
    r1 = (r0 - backcast) * mask
    _, part1, saved1 = plain_forward(blocks[1], r1)
    forecast = part0.astype(jnp.bfloat16).astype(jnp.float32) + part1
    f = adj.astype(jnp.bfloat16)
    zero = jnp.zeros_like(r0)
    da1, grads1 = plain_backward(blocks[1], saved1, (-(zero * mask)).astype(jnp.bfloat16), f)
    dr1 = zero * mask + da1
    t = dr1.astype(jnp.bfloat16).astype(jnp.float32)
    da0, grads0 = plain_backward(blocks[0], saved0, (-(t * mask)).astype(jnp.bfloat16), f)
    dr0 = (t * mask + da0) * mask

    def by_section(first_block, second_block):
        mine, other = (
            jnp.where(core == 0, first_block, second_block),
            jnp.where(core == 0, second_block, first_block),
        )
        got = lax.ppermute(other, "section", [(0, 1), (1, 0)])
        return jnp.where(
            core == 0, jnp.concatenate([mine, got]), jnp.concatenate([got, mine])
        )[None]

    prediction = by_section(part0, forecast)
    sensitivity = by_section(dr0, dr1)
    packed = jnp.stack([unit_rows(*grads0), unit_rows(*grads1)])
    packed = lax.psum_scatter(packed, "section", scatter_dimension=0, tiled=False)
    packed = lax.psum_scatter(packed, "dp", scatter_dimension=0, tiled=True)
    norm = jnp.sqrt(lax.psum(jnp.sum(packed * packed), ("section", "dp")))
    factor = 1.0 / jnp.maximum(norm, 1.0)
    summed = [g[None] for g in from_unit_rows(packed, past, hidden, past + span)]
    updated = [adamw(*four, factor) for four in zip(masters, summed, momenta, variances)]
    return (
        prediction,
        sensitivity,
        norm,
        *summed,
        *(u[0] for u in updated),
        *(u[1] for u in updated),
        *(u[2] for u in updated),
    )


PLANES = {16: (4, 2, 2)}
MESH = pl.DeviceIdType.MESH
MATS = 6
CORE_SLOTS, DIAG_SLOTS, PLAIN_SLOTS, PAIR_SLOTS = 4, 4, 6, 4
BF, F32 = jnp.bfloat16, jnp.float32


def remote(src, dst, send_sem, recv_sem, device):
    return pltpu.make_async_remote_copy(
        src_ref=src, dst_ref=dst, send_sem=send_sem, recv_sem=recv_sem, device_id=device, device_id_type=MESH
    )


def train_kernel(
    sizes,
    seg_hbm, adj_hbm, ext_hbm, first_hbm, square_hbm, head_hbm, biases_hbm,
    pred_out, sens_out, grad_out, norm_out,
    wg, handed, gp, from_core, from_diag, from_plain, from_pair, from_z, total,
    act_t, in_t, theta_keep, slope, work, resid, mask, f_ref, e_t, bias_t, bias_sum, pad,
    seg, adj, ext, first, square, head, biases, part_t, pred, sens, squares, norm_buf,
    own_send, own_recv, ag_send, ag_recv, rs_send, rs_recv, out_send, out_recv, local_sem, norm_send, norm_recv,
):
    ZN, YN, XN, windows, tile, past, span, hidden = sizes
    units = ZN * YN * XN
    core, dp = lax.axis_index("section"), lax.axis_index("dp")
    x, y, z = lax.rem(dp, XN), lax.rem(lax.div(dp, XN), YN), lax.div(dp, XN * YN)
    other, xo, yo = 1 - core, 1 - x, 1 - y
    near_y, near_x = y + core * (yo - y), xo + core * (x - xo)
    far_y, far_x = yo + core * (y - yo), x + core * (xo - x)

    def chip(zi, yi, xi):
        return (core, (zi * YN + yi) * XN + xi)

    sibling = (other, dp)
    z_peers = [lax.rem(z + step, ZN) for step in range(1, ZN)]

    row0 = core * windows
    loads = [
        pltpu.make_async_copy(seg_hbm.at[pl.ds(row0, windows), :], seg, local_sem.at[0]),
        pltpu.make_async_copy(adj_hbm.at[:, pl.ds(row0, windows)], adj, local_sem.at[1]),
    ]
    small_loads = [
        pltpu.make_async_copy(source, target, local_sem.at[4 + n])
        for n, (source, target) in enumerate(
            [(square_hbm, square), (first_hbm, first), (head_hbm, head), (biases_hbm, biases), (ext_hbm, ext)]
        )
    ]
    for load in small_loads + loads:
        load.start()

    barrier = pltpu.get_barrier_semaphore()
    plane_peers = [
        (ci, (z * YN + yi) * XN + xi) for ci in (core, other) for yi in (y, yo) for xi in (x, xo)
    ][1:]
    peers = plane_peers + [chip(zi, y, x) for zi in z_peers]
    for peer in peers:
        pl.semaphore_signal(barrier, inc=1, device_id=peer, device_id_type=MESH)

    rows = hidden // units
    half_rows = rows // 2

    def put_own(m, value, lanes):
        halves = value.astype(BF).reshape(2, half_rows, -1)
        for h in range(2):
            pl.when(core == h)(functools.partial(put_half, m, halves[h], halves[1 - h], lanes))

    def put_half(m, kept, given, lanes):
        wg[core, m, z, y, x, core, :, lanes] = kept
        handed[m, :, lanes] = given

    for load in small_loads:
        load.wait()
    pad[...] = jnp.zeros_like(pad)
    pad[0:rows, 0:past] = first[0] * 0.5
    put_own(0, pad[0:rows, :], slice(0, 128))
    pad[...] = jnp.zeros_like(pad)
    pad[span : span + 4, 0:rows] = biases[0] * 0.5
    bias_cols = pad[...].T[0:rows]
    pad[...] = jnp.zeros_like(pad)
    pad[0:rows, 0:span] = head[0, :, past : past + span]
    put_own(0, pad[0:rows, :] + bias_cols, slice(128, 256))
    pad[...] = jnp.zeros_like(pad)
    pad[0:rows, 0:past] = head[0, :, 0:past]
    put_own(0, pad[0:rows, :], slice(256, 384))
    pl.semaphore_wait(barrier, len(peers))

    def hand_over(m, lanes):
        return remote(
            handed.at[m, :, lanes], wg.at[core, m, z, y, x, other, :, lanes], own_send.at[m], own_recv.at[m], sibling
        )

    hand_over(0, slice(0, 384)).start()
    for m in range(1, MATS):
        put_own(m, square[0, m - 1] * 0.5 if m < 4 else square[0, m - 1], slice(0, hidden))
        hand_over(m, slice(0, hidden)).start()


    def of(i):
        b = jnp.where(jnp.logical_and(i >= 5, i <= 10), 1, 0)
        return b, jnp.where(i <= 4, i, jnp.where(i <= 10, i - 5, 5))

    def sends(sems, kind, lanes):
        return sems.at[kind, 0 if lanes.stop == hidden else 1]

    def z_copies(i, lanes):
        b, m = of(i)
        part = wg.at[b, m, z, y, x, core, :, lanes]
        return [
            remote(part, part, sends(ag_send, 0, lanes), ag_recv.at[i, s], chip(zi, y, x)) for s, zi in enumerate(z_peers)
        ]

    def column_copies(i, lanes):
        b, m = of(i)
        part = wg.at[b, m, :, y, x, core, :, lanes]
        return [
            remote(part, part, sends(ag_send, 1, lanes), ag_recv.at[i, 3], chip(z, near_y, near_x)),
            remote(part, part, sends(ag_send, 1, lanes), ag_recv.at[i, 4], chip(z, far_y, far_x)),
        ]

    def corner_copy(i, lanes):
        b, m = of(i)
        part = wg.at[b, m, :, near_y, near_x, core, :, lanes]
        return remote(part, part, sends(ag_send, 2, lanes), ag_recv.at[i, 5], chip(z, far_y, far_x))

    def core_copy(i, lanes):
        b, m = of(i)
        part = wg.at[b, m, :, :, :, core, :, lanes]
        return remote(part, part, sends(ag_send, 3, lanes), ag_recv.at[i, 6], sibling)

    def by_lanes(m, step):
        pl.when(m == 0)(lambda: step(slice(0, 384)))
        pl.when(m > 0)(lambda: step(slice(0, hidden)))

    def start_all(copies):
        for copy in copies:
            copy.start()

    for load in loads:
        load.wait()
    zeros_tile = jnp.zeros((tile, 128), F32)

    def prepare(t, carry):
        at = pl.ds(t * tile, tile)
        resid[at, :] = zeros_tile
        resid[at, 0:past] = seg[at, :]
        return carry

    def prepare_mask(g, carry):
        lengths = ext[pl.ds(core * (windows // 128) + g, 1), :]
        position = lax.broadcasted_iota(jnp.int32, (128, 128), 0)
        keep = jnp.where(position >= past - lengths, 1.0, 0.0).astype(F32).T
        at = pl.ds(pl.multiple_of(g * 128, 128), 128)
        pad[0:span, :] = adj[:, at]
        f_ref[at, :] = pad[...].T.astype(BF)
        mask[at, :] = keep.astype(BF)
        resid[at, :] = resid[at, :] * keep
        return carry

    tiles = windows // tile
    part_tile = windows // 2

    def matrix(b, m):
        return wg[b, m].reshape(hidden, hidden)

    def small(b, lane):
        return wg[b, 0, :, :, :, :, :, lane : lane + 128].reshape(hidden, 128)

    def store_layer(b, k, at, v):
        p = 1.0 + jnp.tanh(v)
        a = v * p
        rate = p + a * (2.0 - p)
        slope[b, k, at, :] = rate.astype(BF)
        low = a.astype(BF)
        act_t[b, k, :, at] = low.T
        return low

    def halves(body):
        for t in range(2):
            body(slice(t * windows // 2, (t + 1) * windows // 2))

    def layer_zero(b):
        bias_t[...] = small(b, 128).astype(F32).T

        def body(at):
            a = resid[at, :].astype(BF)
            in_t[b, :, at] = a.T
            work[0, at, :] = store_layer(b, 0, at, dot_nt(a, small(b, 0)) + bias_t[span : span + 1, :])

        halves(body)

    def layer_next(b, k):
        source, target = lax.rem(k + 1, 2), lax.rem(k, 2)
        v = dot_nn(work[source], matrix(b, k)) + bias_t[pl.ds(span + k, 1), :]
        work[target] = store_layer(b, k, slice(0, windows), v)

    def grid(value):
        return value.astype(BF).reshape(ZN, YN, XN, 2, half_rows, -1)

    def backcast_step():
        def body(at):
            theta = dot_nn(work[1, at, :], matrix(0, 4)).astype(BF)
            theta_keep[at, :] = theta
            resid[at, :] = (resid[at, :] - dot_nn(theta, small(0, 256))) * mask[at, :].astype(F32)

        halves(body)

    def put_rows(buf, b, at, value):
        for row in range(value.shape[0]):
            buf[b, row, :, at] = value[row : row + 1]

    def late_theta(b, m):
        theta_t = act_t.at[1, 0]
        theta_t[...] = dot_nn(matrix(b, m).T, act_t[b, 3]).astype(BF)

        @pl.when(m == 4)
        def _():
            gp[b, 0, :, :, :, :, :, 256:384] = grid(dot_nt(theta_t[...], e_t[b]))

        @pl.when(m == 5)
        def _():
            grad = grid(dot_nn(theta_t[...], f_ref[...]))
            gp[b, 0, :, :, :, :, :, 128:256] = gp[b, 0, :, :, :, :, :, 128:256] + grad
            part_t[b] = dot_nn(small(b, 128).T, theta_t[...])[0:span]

    def forecasts():
        put_rows(pred, 0, slice(0, windows), part_t[0])
        put_rows(pred, 1, slice(0, windows), part_t[0].astype(BF).astype(F32) + part_t[1])

    count = 2 * MATS

    def delayed(lag, t, step):
        pl.when(jnp.logical_and(t >= lag, t < count + lag))(lambda: step(t - lag))

    def staged(lag, t, step):
        early = t - lag + 1
        pl.when(jnp.logical_and(early >= 1, early <= 2))(lambda: step(early))
        unit = t - lag
        pl.when(jnp.logical_and(unit >= 3, unit < count))(lambda: step(unit))
        if lag == 6:
            pl.when(t == 3)(lambda: step(0))

    def gather_line(i):
        b, m = of(i)

        def step(lanes):
            pl.when(b != core)(lambda: hand_over(m, lanes).wait_recv())
            start_all(z_copies(i, lanes))

        by_lanes(m, step)

    def gather_columns(i):
        def step(lanes):
            for copy in z_copies(i, lanes):
                copy.wait_recv()
            start_all(column_copies(i, lanes))

        by_lanes(of(i)[1], step)

    def gather_corner(i):
        def step(lanes):
            column_copies(i, lanes)[0].wait_recv()
            corner_copy(i, lanes).start()

        by_lanes(of(i)[1], step)

    def gather_core(i):
        def step(lanes):
            column_copies(i, lanes)[1].wait_recv()
            corner_copy(i, lanes).wait_recv()
            core_copy(i, lanes).start()

        by_lanes(of(i)[1], step)

    def arrived(i):
        by_lanes(of(i)[1], lambda lanes: core_copy(i, lanes).wait_recv())

    def forward_unit(i):
        arrived(i)
        b, m = of(i)
        pl.when(m == 0)(lambda: layer_zero(b))
        pl.when(jnp.logical_and(m >= 1, m <= 3))(lambda: layer_next(b, m))
        pl.when(m == 4)(backcast_step)

        @pl.when(jnp.logical_or(i == 4, i == 8))
        def _():
            pl.when(b == 1)(lambda: feed(b))
            pl.when(b == 0)(lambda: feed_forward(b))
            lax.fori_loop(jnp.where(b == 1, 4, 5), MATS, lambda n, carry: (theta_grad(b, n), carry)[1], 0)
            pl.when(b == 0)(lambda: scatter_start(0))

            @pl.when(b == 1)
            def _():
                scatter_start(1)
                scatter_start(2)

    def gather_step(t, carry):
        pl.when(t == 12)(lambda: scatter_core(0))
        pl.when(t == 15)(lambda: scatter_diag(0))
        delayed(4, t, gather_core)
        delayed(2, t, gather_corner)
        delayed(0, t, gather_columns)
        pl.when(t + 4 < count)(lambda: gather_line(t + 4))
        pl.when(jnp.logical_and(t >= 5, t < 14))(lambda: forward_unit(t - 5))
        return carry

    def out_copies(buf, out, s):
        at = pl.ds(row0, windows)
        return [
            pltpu.make_async_copy(buf.at[core], out.at[:, :, at], local_sem.at[2 + s]),
            remote(buf.at[other], out.at[:, :, at], out_send.at[s], out_recv.at[s], sibling),
        ]


    def back_of(j):
        b = jnp.where(jnp.logical_or(jnp.logical_and(j >= 1, j <= 5), j == 10), 1, 0)
        early = jnp.where(j == 1, 4, jnp.where(j <= 2, 5, 6 - j))
        return b, jnp.where(j <= 5, early, jnp.where(j == 6, 4, jnp.where(j <= 9, 10 - j, 0)))

    def to_core(j, lanes):
        b, m = back_of(j)
        return remote(
            gp.at[b, m, :, :, :, other, :, lanes], from_core.at[lax.rem(j, CORE_SLOTS), :, :, :, :, lanes],
            sends(rs_send, 3, lanes), rs_recv.at[j, 0], sibling,
        )

    def to_far(j, lanes):
        b, m = back_of(j)
        device = chip(z, far_y, far_x)
        return [
            remote(
                gp.at[b, m, :, yo, xo, core, :, lanes], from_diag.at[lax.rem(j, DIAG_SLOTS), :, :, lanes],
                sends(rs_send, 1, lanes), rs_recv.at[j, 1], device,
            ),
            remote(
                gp.at[b, m, :, far_y, far_x, core, :, lanes], from_plain.at[lax.rem(j, PLAIN_SLOTS), :, :, lanes],
                sends(rs_send, 1, lanes), rs_recv.at[j, 2], device,
            ),
        ]

    def to_near(j, lanes):
        b, m = back_of(j)
        return remote(
            gp.at[b, m, :, near_y, near_x, core, :, lanes], from_pair.at[lax.rem(j, PAIR_SLOTS), :, :, lanes],
            sends(rs_send, 2, lanes), rs_recv.at[j, 3], chip(z, near_y, near_x),
        )

    def to_z(j, lanes):
        b, m = back_of(j)
        return [
            remote(
                gp.at[b, m, zi, y, x, core, :, lanes], from_z.at[j, s, :, lanes],
                sends(rs_send, 0, lanes), rs_recv.at[j, 4 + s], chip(zi, y, x),
            )
            for s, zi in enumerate(z_peers)
        ]

    def scatter_start(j):
        by_lanes(back_of(j)[1], lambda lanes: to_core(j, lanes).start())

    def scatter_core(j):
        b, m = back_of(j)

        def step(lanes):
            to_core(j, lanes).wait_recv()
            part = gp[b, m, :, :, :, core, :, lanes] + from_core[lax.rem(j, CORE_SLOTS), :, :, :, :, lanes]
            gp[b, m, :, :, :, core, :, lanes] = part
            start_all(to_far(j, lanes))

        by_lanes(m, step)

    def scatter_diag(j):
        b, m = back_of(j)

        def step(lanes):
            to_far(j, lanes)[0].wait_recv()
            part = gp[b, m, :, near_y, near_x, core, :, lanes] + from_diag[lax.rem(j, DIAG_SLOTS), :, :, lanes]
            gp[b, m, :, near_y, near_x, core, :, lanes] = part
            to_near(j, lanes).start()

        by_lanes(m, step)

    def scatter_plane(j):
        b, m = back_of(j)

        def step(lanes):
            to_far(j, lanes)[1].wait_recv()
            to_near(j, lanes).wait_recv()
            value = gp[b, m, :, y, x, core, :, lanes].astype(F32)
            value = value + from_plain[lax.rem(j, PLAIN_SLOTS), :, :, lanes].astype(F32)
            value = value + from_pair[lax.rem(j, PAIR_SLOTS), :, :, lanes].astype(F32)
            gp[b, m, :, y, x, core, :, lanes] = value.astype(BF)
            start_all(to_z(j, lanes))

        by_lanes(m, step)

    def scatter_z(j):
        b, m = back_of(j)

        def step(lanes):
            for copy in to_z(j, lanes):
                copy.wait_recv()
            value = gp[b, m, z, y, x, core, :, lanes].astype(F32)
            for s in range(ZN - 1):
                value = value + from_z[j, s, :, lanes].astype(F32)
            total[b, m, :, lanes] = value
            squares[:, lanes] = squares[:, lanes] + value * value

        by_lanes(m, step)

    def add_rows(value):
        return jnp.sum(value.reshape(-1, 8, hidden), axis=0)

    def put_bias(k, acc):
        bias_sum[pl.ds(span + k, 1), :] = jnp.sum(acc, axis=0, keepdims=True)

    def feed(b):
        pl.when(b == 1)(lambda: resid.__setitem__(..., jnp.zeros_like(resid)))
        e = (-(resid[...] * mask[...].astype(F32))).astype(BF)
        e_t[b] = e.T
        work[0] = dot_nt(e, small(b, 256)).astype(BF)
        work[2] = dot_nt(f_ref[...], small(b, 128)).astype(BF)

    def feed_forward(b):
        work[2] = dot_nt(f_ref[...], small(b, 128)).astype(BF)

    def put_dz(b, k, da):
        dz = da * slope[b, k].astype(F32)
        work[k % 2 if isinstance(k, int) else lax.rem(k, 2)] = dz.astype(BF)
        bias_sum[pl.ds(span + k, 1), :] = jnp.sum(add_rows(dz), axis=0, keepdims=True)

    def theta_step(b):
        put_dz(b, 3, 0.5 * (dot_nt(work[0], matrix(b, 4)) + dot_nt(work[2], matrix(b, 5))))

    def layer_back(b, k):
        source = lax.rem(k, 2)
        gp[b, k] = grid(dot_nn(act_t[b, k - 1], work[source]))
        put_dz(b, k - 1, dot_nt(work[source], matrix(b, k)))

    def theta_grad(b, m):
        gp[b, m] = grid(dot_nn(act_t[b, 3], work[jnp.where(m == 4, 0, 2)]))

    def first_grads(b):
        gp[b, 0, :, :, :, :, :, 0:128] = grid(dot_nn(in_t[b], work[0]).T)
        gp[b, 0, :, :, :, :, :, 128:256] = grid(bias_sum[...].T)
        pl.when(b == 0)(backcast_grad)

    def backcast_grad():
        gp[0, 0, :, :, :, :, :, 256:384] = grid(dot_nn(e_t[0], theta_keep[...]).T)

    def input_grad(b):
        for t in range(2):
            at = slice(t * windows // 2, (t + 1) * windows // 2)
            keep = mask[at, :].astype(F32)
            dr = resid[at, :] * keep + 2.0 * dot_nn(work[0, at, :], small(b, 0))

            @pl.when(b == 1)
            def _():
                seg[at, :] = dr[:, 0:past]
                resid[at, :] = dr.astype(BF).astype(F32)

            @pl.when(b == 0)
            def _():
                put_rows(sens, 0, at, (dr * keep).T[0:past])

    def late_rows():
        for g in range(windows // 128):
            at = slice(g * 128, (g + 1) * 128)
            pad[:, 0:past] = seg[at, :]
            put_rows(sens, 1, at, pad[...].T[0:past])

    bias_sum[...] = jnp.zeros_like(bias_sum)
    squares[...] = jnp.zeros_like(squares)
    total[...] = jnp.zeros_like(total)

    def back_step(j, carry):
        b, m = back_of(j)

        @pl.when(jnp.logical_and(j >= count, j < count + 4))
        def _():
            scatter_z(2 * (j - count))
            scatter_z(2 * (j - count) + 1)

        pl.when(j >= count + 4)(lambda: scatter_z(j - 8))
        staged(6, j, scatter_plane)
        staged(4, j, scatter_diag)
        staged(2, j, scatter_core)

        @pl.when(j == 2)
        def _():
            arrived(9)
            arrived(10)
            theta_step(1)

        pl.when(jnp.logical_and(m >= 1, m <= 3))(lambda: layer_back(b, m))

        @pl.when(jnp.logical_or(j == 6, j == count - 1))
        def _():
            block = jnp.where(j == 6, 1, 0)
            first_grads(block)
            pl.when(j == 6)(lambda: input_grad(1))

        @pl.when(j == 6)
        def _():
            feed(0)
            theta_grad(0, 4)

        @pl.when(jnp.logical_or(j == 10, j == 11))
        def _():
            lax.fori_loop(jnp.where(j == 10, 4, 5), MATS, lambda n, carry: (late_theta(b, n), carry)[1], 0)

        pl.when(jnp.logical_and(j >= 3, j < count))(lambda: scatter_start(j))

        @pl.when(j == 6)
        def _():
            arrived(11)
            theta_step(0)

        @pl.when(j == count - 1)
        def _():
            input_grad(0)
            forecasts()
            start_all(out_copies(pred, pred_out, 0))

        @pl.when(j == count)
        def _():
            late_rows()
            start_all(out_copies(sens, sens_out, 1))

        return carry

    for i in range(4):
        gather_line(i)
    lax.fori_loop(0, tiles, prepare, 0)
    pad[...] = jnp.zeros_like(pad)
    lax.fori_loop(0, windows // 128, prepare_mask, 0)
    lax.fori_loop(0, count + 4, gather_step, 0)

    lax.fori_loop(2, count + 8, back_step, 0)

    grad_copy = remote(total.at[other], grad_out.at[:, core], out_send.at[2], out_recv.at[2], sibling)
    grad_copy.start()
    grad_out[:, core] = total[core]
    sq = squares[:, 0:128] + squares[:, 128:256] + squares[:, 256:384] + squares[:, 384:512]
    place = (y * XN + x) * 2 + core
    norm_buf[place] = sq[0:8] + sq[8:16]

    def spread(sources, targets, first):
        copies = [
            remote(norm_buf.at[sources], norm_buf.at[sources], norm_send.at[first + s], norm_recv.at[first + s], device)
            for s, device in enumerate(targets)
        ]
        start_all(copies)
        for copy in copies:
            copy.wait()

    def add_up(slots):
        value = norm_buf[slots[0]]
        for slot in slots[1:]:
            value = value + norm_buf[slot]
        return value

    spread(place, plane_peers, 0)
    norm_buf[8 + z] = add_up(range(8))
    spread(8 + z, [chip(zi, y, x) for zi in z_peers], 7)
    everything = add_up(range(8, 8 + ZN))
    norm_out[...] = jnp.broadcast_to(jnp.sqrt(jnp.sum(everything, keepdims=True)), norm_out.shape)

    grad_copy.wait()
    for buf, out, s in ((pred, pred_out, 0), (sens, sens_out, 1)):
        for copy in out_copies(buf, out, s):
            copy.wait()
    for m in range(MATS):
        hand_over(m, slice(0, hidden if m else 384)).wait_send()

    for mats, lanes in ((slice(1, MATS), slice(0, hidden)), (slice(0, 1), slice(0, 384))):
        sent = (
            wg.at[:, mats, 0 : ZN - 1, 0, 0, 0, :, lanes],
            wg.at[:, mats, :, :, 0, 0, :, lanes],
            wg.at[:, mats, :, 0, 0, 0, :, lanes],
            wg.at[:, mats, :, :, :, 0, :, lanes],
        )
        for sems in (ag_send, rs_send):
            for kind, ref in enumerate(sent):
                remote(ref, ref, sends(sems, kind, lanes), out_recv.at[0], sibling).wait_send()


def train_call(plane, segments, extents, adjoint, first, square, head, biases):
    ZN, YN, XN = plane
    past, span, hidden = segments.shape[1], adjoint.shape[0], square.shape[3]
    windows = segments.shape[0] // 2
    tile = windows
    half = hidden // (ZN * YN * XN) // 2
    sizes = (ZN, YN, XN, windows, tile, past, span, hidden)
    DMA = pltpu.SemaphoreType.DMA
    vmem = pl.BlockSpec(memory_space=pltpu.VMEM)
    hbm = pl.BlockSpec(memory_space=pl.ANY)
    count = 2 * MATS
    flops = 2 * 2 * 3 * windows * hidden * (6 * hidden + 2 * 128)
    lengths = extents.reshape(-1, 128)
    return pl.pallas_call(
        functools.partial(train_kernel, sizes),
        out_shape=(
            jax.ShapeDtypeStruct((span, 1, 2 * windows), F32),
            jax.ShapeDtypeStruct((past, 1, 2 * windows), F32),
            jax.ShapeDtypeStruct((MATS, 2, half, hidden), F32),
            jax.ShapeDtypeStruct((8, 128), F32),
        ),
        in_specs=[hbm] * 7,
        out_specs=(hbm, hbm, vmem, vmem),
        scratch_shapes=[
            pltpu.VMEM((2, MATS, ZN, YN, XN, 2, half, hidden), BF),
            pltpu.VMEM((MATS, half, hidden), BF),
            pltpu.VMEM((2, MATS, ZN, YN, XN, 2, half, hidden), BF),
            pltpu.VMEM((CORE_SLOTS, ZN, YN, XN, half, hidden), BF),
            pltpu.VMEM((DIAG_SLOTS, ZN, half, hidden), BF),
            pltpu.VMEM((PLAIN_SLOTS, ZN, half, hidden), BF),
            pltpu.VMEM((PAIR_SLOTS, ZN, half, hidden), BF),
            pltpu.VMEM((count, ZN - 1, half, hidden), BF),
            pltpu.VMEM((2, MATS, half, hidden), F32),
            pltpu.VMEM((2, 4, hidden, windows), BF),
            pltpu.VMEM((2, 128, windows), BF),
            pltpu.VMEM((windows, hidden), BF),
            pltpu.VMEM((2, 4, windows, hidden), BF),
            pltpu.VMEM((3, windows, hidden), BF),
            pltpu.VMEM((windows, 128), F32),
            pltpu.VMEM((windows, 128), BF),
            pltpu.VMEM((windows, 128), BF),
            pltpu.VMEM((2, 128, windows), BF),
            pltpu.VMEM((128, hidden), F32),
            pltpu.VMEM((128, hidden), F32),
            pltpu.VMEM((128, 128), F32),
            pltpu.VMEM((windows, past), F32),
            pltpu.VMEM((span, windows), F32),
            *(pltpu.VMEM(a.shape, a.dtype) for a in (lengths, first, square, head, biases)),
            pltpu.VMEM((2, span, windows), F32),
            pltpu.VMEM((2, span, 1, windows), F32),
            pltpu.VMEM((2, past, 1, windows), F32),
            pltpu.VMEM((half, hidden), F32),
            pltpu.VMEM((8 + ZN, 8, 128), F32),
            DMA((MATS,)),
            DMA((MATS,)),
            DMA((4, 2)),
            DMA((count, 4 + ZN - 1)),
            DMA((4, 2)),
            DMA((count, 4 + ZN - 1)),
            DMA((3,)),
            DMA((3,)),
            DMA((9,)),
            DMA((7 + ZN - 1,)),
            DMA((7 + ZN - 1,)),
        ],
        compiler_params=pltpu.CompilerParams(
            collective_id=0, has_side_effects=True, vmem_limit_bytes=64 * 1024 * 1024
        ),
        cost_estimate=pl.CostEstimate(flops=flops, bytes_accessed=8_000_000, transcendentals=8 * windows * hidden),
        name="train",
    )(segments, adjoint, lengths, first, square, head, biases)


def update_kernel(past, span, *refs):
    sources, targets, norm_out = refs[0:16], refs[16:34], refs[34]
    held, results, pad, in_sem, out_sem = refs[35:51], refs[51:67], *refs[67:70]
    arriving = [pltpu.make_async_copy(source, ref, in_sem.at[n]) for n, (source, ref) in enumerate(zip(sources, held))]
    leaving = [
        pltpu.make_async_copy(ref, target, out_sem.at[n]) for n, (ref, target) in enumerate(zip(held[0:2] + results, targets))
    ]
    for copy in arriving:
        copy.start()
    grads, norm, masters, momenta, variances = held[2], held[3], held[4:8], held[8:12], held[12:16]
    units = masters[3].shape[2]

    def rows(m, lane, width):
        return grads[m, :, :, lane : lane + width].reshape(units, width)

    arriving[2].wait()
    arriving[3].wait()
    norm_out[...] = norm[0:1, 0:1]
    factor = 1.0 / jnp.maximum(norm[0:1, 0:1], 1.0)
    for m in range(5):
        results[1][0, m] = rows(m + 1, 0, grads.shape[3])
    results[0][0] = rows(0, 0, 128)[:, 0:past]
    forecast = rows(0, 128, 128)
    pad[...] = jnp.zeros_like(pad)
    pad[0:units, :] = forecast
    results[3][0] = pad[...].T[span : span + 4, 0:units]
    results[2][0, :, 0:past] = rows(0, 256, 128)[:, 0:past]
    results[2][0, :, past : past + span] = forecast[:, 0:span]
    for n in (0, 1):
        arriving[n].wait()
        leaving[n].start()
    for n in (1, 0, 2, 3):
        leaving[2 + n].start()
        for state in range(3):
            arriving[4 + 4 * state + n].wait()
        updated = adamw(masters[n][...], results[n][...], momenta[n][...], variances[n][...], factor[None])
        for kind, value in enumerate(updated):
            results[4 * (kind + 1) + n][...] = value
            leaving[2 + 4 * (kind + 1) + n].start()
    for copy in leaving:
        copy.wait()


def update_call(prediction, sensitivity, grads, norm, state):
    hbm = pl.BlockSpec(memory_space=pl.ANY)
    sources = (prediction, sensitivity, grads, norm, *state)
    targets = (prediction, sensitivity, *(4 * list(state[:4])))
    return pl.pallas_call(
        functools.partial(update_kernel, sensitivity.shape[0], prediction.shape[0]),
        out_shape=tuple(jax.ShapeDtypeStruct(a.shape, F32) for a in targets) + (jax.ShapeDtypeStruct((1, 1), F32),),
        in_specs=[hbm] * len(sources),
        out_specs=tuple([hbm] * len(targets) + [pl.BlockSpec(memory_space=pltpu.VMEM)]),
        scratch_shapes=[pltpu.VMEM(a.shape, F32) for a in sources]
        + [pltpu.VMEM(a.shape, F32) for a in targets[2:]]
        + [pltpu.VMEM((128, 128), F32), pltpu.SemaphoreType.DMA((len(sources),)), pltpu.SemaphoreType.DMA((len(targets),))],
        name="update",
    )(*sources)


def turned(arrays):
    return [a.transpose(0, 2, 1) if n % 4 == 0 else a for n, a in enumerate(arrays)]


def kernel_shards(plane, segments, extents, adjoint, *state):
    state = turned(state)
    results = train_call(plane, segments, extents, adjoint.T, *state[:4])
    prediction, sensitivity, *updated, norm = update_call(*results, state)
    by_window = (prediction.transpose(1, 2, 0), sensitivity.transpose(1, 2, 0))
    return (*by_window, norm.reshape(()), *turned(updated))


STATE_SPECS = (
    P("section", None, "dp"),
    P("section", None, "dp", None),
    P("section", "dp", None),
    P("section", None, "dp"),
)


def solution(mesh):
    in_specs = (P("dp", None), P("dp"), P("dp", None)) + 3 * STATE_SPECS
    out_specs = (P("section", "dp", None), P("section", "dp", None), P()) + 4 * STATE_SPECS
    plane = PLANES.get(mesh.shape["dp"])
    shards = plain_shards if plane is None else functools.partial(kernel_shards, plane)
    return jax.shard_map(shards, mesh=mesh, in_specs=in_specs, out_specs=out_specs, check_vma=False)
```

profile of v0, /device:TPU:0, one launch (start us, length us, event | category | flops | bytes accessed | tf_op | source)
XLA Modules:
  0.0 98.1 jit_solution(15016031091304718163)
XLA Ops:
  0.7 92.9 %train.1 = (f32[18,1,3072]{2,1,0:T(1,128)}, f32[126,1,3072]{2,1,0:T(1,128)}, f32[6,2,16,512]{3,2,1,0:T(8,128)}, f32[8,128]{1,0:T(8,128)}) custom-call(f32[3072,126]{1,0:T(8,128)} %seg_hbm.1, f32[18,3072]{1,0:T(8,128)} %bitcast.17, s32[24,128]{1,0:T(8,128)} %bitcast.23, f32[1,32,126]{2,1,0:T(8,128)} %bitcast.12, f32[1,5,32,512]{3,2,1,0:T(8,128)} %refs_5_.1, ...), custom_call_target="tpu_custom_call" | custom-call | flops 31406948352 | bytes 8000000 | tf_op jit(solution)/shard_map/train/pallas_call | solution.py:747
  93.6 4.4 %update.1 = (f32[18,1,3072]{2,1,0:T(1,128)}, f32[126,1,3072]{2,1,0:T(1,128)}, f32[1,32,126]{2,1,0:T(8,128)}, f32[1,5,32,512]{3,2,1,0:T(8,128)}, f32[1,32,144]{2,...) custom-call(f32[18,1,3072]{2,1,0:T(1,128)} %get-tuple-element.42.ref, ...), custom_call_target="tpu_custom_call" | custom-call | tf_op jit(solution)/shard_map/update/pallas_call | solution.py:854
where the time goes:
time: 98.2 us; the launch traced here: 98.1 us
  Pallas kernels  97.2 us (99%)
    pallas_call x1, Pallas kernels, train_call(): pl.pallas_call(functools.partial(train_kernel, sizes), out_shape=(jax.Sha...  92.9 us
    pallas_call x1, Pallas kernels, update_call(): pl.pallas_call(functools.partial(update_kernel, sensitivity.shape[0], pre...  4.35 us

commit v1 on v0

--- a/solution.py
+++ b/solution.py
@@ -152,6 +152,9 @@
 BF, F32 = jnp.bfloat16, jnp.float32
 
 
+ORDER = ((0, 5), (1, 4), (1, 5), (1, 3), (1, 2), (1, 1), (0, 4), (0, 3), (0, 2), (0, 1), (1, 0), (0, 0))
+
+
 def remote(src, dst, send_sem, recv_sem, device):
     return pltpu.make_async_remote_copy(
         src_ref=src, dst_ref=dst, send_sem=send_sem, recv_sem=recv_sem, device_id=device, device_id_type=MESH
@@ -199,7 +202,7 @@
     plane_peers = [
         (ci, (z * YN + yi) * XN + xi) for ci in (core, other) for yi in (y, yo) for xi in (x, xo)
     ][1:]
-    peers = plane_peers + [chip(zi, y, x) for zi in z_peers]
+    peers = plane_peers + [(ci, (zi * YN + y) * XN + x) for zi in z_peers for ci in (core, other)]
     for peer in peers:
         pl.semaphore_signal(barrier, inc=1, device_id=peer, device_id_type=MESH)
 
@@ -236,10 +239,8 @@
             handed.at[m, :, lanes], wg.at[core, m, z, y, x, other, :, lanes], own_send.at[m], own_recv.at[m], sibling
         )
 
-    hand_over(0, slice(0, 384)).start()
-    for m in range(1, MATS):
+    def pack(m):
         put_own(m, square[0, m - 1] * 0.5 if m < 4 else square[0, m - 1], slice(0, hidden))
-        hand_over(m, slice(0, hidden)).start()
 
 
     def of(i):
@@ -254,6 +255,16 @@
         part = wg.at[b, m, z, y, x, core, :, lanes]
         return [
             remote(part, part, sends(ag_send, 0, lanes), ag_recv.at[i, s], chip(zi, y, x)) for s, zi in enumerate(z_peers)
+        ]
+
+    def line_copies(i, lanes):
+        b, m = of(i)
+        given = wg.at[b, m, z, y, x, other, :, lanes]
+        return [
+            remote(
+                handed.at[m, :, lanes], given, sends(ag_send, 0, lanes), ag_recv.at[i, s], (other, (zi * YN + y) * XN + x)
+            )
+            for s, zi in enumerate(z_peers)
         ]
 
     def column_copies(i, lanes):
@@ -275,6 +286,9 @@
         return remote(part, part, sends(ag_send, 3, lanes), ag_recv.at[i, 6], sibling)
 
     def by_lanes(m, step):
+        if isinstance(m, int):
+            step(slice(0, hidden if m else 384))
+            return
         pl.when(m == 0)(lambda: step(slice(0, 384)))
         pl.when(m > 0)(lambda: step(slice(0, hidden)))
 
@@ -282,8 +296,6 @@
         for copy in copies:
             copy.start()
 
-    for load in loads:
-        load.wait()
     zeros_tile = jnp.zeros((tile, 128), F32)
 
     def prepare(t, carry):
@@ -380,7 +392,7 @@
 
     def staged(lag, t, step):
         early = t - lag + 1
-        pl.when(jnp.logical_and(early >= 1, early <= 2))(lambda: step(early))
+        pl.when(jnp.logical_and(early >= (2 if lag == 2 else 1), early <= 2))(lambda: step(early))
         unit = t - lag
         pl.when(jnp.logical_and(unit >= 3, unit < count))(lambda: step(unit))
         if lag == 6:
@@ -389,19 +401,18 @@
     def gather_line(i):
         b, m = of(i)
 
+        pl.when(b == core)(lambda: by_lanes(m, lambda lanes: start_all(line_copies(i, lanes) + z_copies(i, lanes))))
+
+    def gather_columns(i):
+        b, m = of(i)
+
         def step(lanes):
             pl.when(b != core)(lambda: hand_over(m, lanes).wait_recv())
-            start_all(z_copies(i, lanes))
-
-        by_lanes(m, step)
-
-    def gather_columns(i):
-        def step(lanes):
             for copy in z_copies(i, lanes):
                 copy.wait_recv()
             start_all(column_copies(i, lanes))
 
-        by_lanes(of(i)[1], step)
+        by_lanes(m, step)
 
     def gather_corner(i):
         def step(lanes):
@@ -428,6 +439,8 @@
         pl.when(jnp.logical_and(m >= 1, m <= 3))(lambda: layer_next(b, m))
         pl.when(m == 4)(backcast_step)
 
+        pl.when(i == 8)(lambda: gather_core(10))
+
         @pl.when(jnp.logical_or(i == 4, i == 8))
         def _():
             pl.when(b == 1)(lambda: feed(b))
@@ -443,10 +456,19 @@
     def gather_step(t, carry):
         pl.when(t == 12)(lambda: scatter_core(0))
         pl.when(t == 15)(lambda: scatter_diag(0))
-        delayed(4, t, gather_core)
+        pl.when(jnp.logical_and(t >= 4, t != 14))(lambda: gather_core(t - 4))
         delayed(2, t, gather_corner)
         delayed(0, t, gather_columns)
         pl.when(t + 4 < count)(lambda: gather_line(t + 4))
+
+        @pl.when(t == 0)
+        def _():
+            for load in loads:
+                load.wait()
+            lax.fori_loop(0, tiles, prepare, 0)
+            pad[...] = jnp.zeros_like(pad)
+            lax.fori_loop(0, windows // 128, prepare_mask, 0)
+
         pl.when(jnp.logical_and(t >= 5, t < 14))(lambda: forward_unit(t - 5))
         return carry
 
@@ -459,6 +481,8 @@
 
 
     def back_of(j):
+        if isinstance(j, int):
+            return ORDER[j]
         b = jnp.where(jnp.logical_or(jnp.logical_and(j >= 1, j <= 5), j == 10), 1, 0)
         early = jnp.where(j == 1, 4, jnp.where(j <= 2, 5, 6 - j))
         return b, jnp.where(j <= 5, early, jnp.where(j == 6, 4, jnp.where(j <= 9, 10 - j, 0)))
@@ -622,12 +646,6 @@
     def back_step(j, carry):
         b, m = back_of(j)
 
-        @pl.when(jnp.logical_and(j >= count, j < count + 4))
-        def _():
-            scatter_z(2 * (j - count))
-            scatter_z(2 * (j - count) + 1)
-
-        pl.when(j >= count + 4)(lambda: scatter_z(j - 8))
         staged(6, j, scatter_plane)
         staged(4, j, scatter_diag)
         staged(2, j, scatter_core)
@@ -637,6 +655,7 @@
             arrived(9)
             arrived(10)
             theta_step(1)
+            scatter_core(1)
 
         pl.when(jnp.logical_and(m >= 1, m <= 3))(lambda: layer_back(b, m))
 
@@ -662,27 +681,37 @@
             arrived(11)
             theta_step(0)
 
-        @pl.when(j == count - 1)
-        def _():
-            input_grad(0)
-            forecasts()
-            start_all(out_copies(pred, pred_out, 0))
-
-        @pl.when(j == count)
-        def _():
-            late_rows()
-            start_all(out_copies(sens, sens_out, 1))
-
         return carry
 
-    for i in range(4):
-        gather_line(i)
-    lax.fori_loop(0, tiles, prepare, 0)
-    pad[...] = jnp.zeros_like(pad)
-    lax.fori_loop(0, windows // 128, prepare_mask, 0)
+    def last_steps():
+        scatter_plane(6), scatter_diag(8), scatter_core(10)
+        input_grad(0)
+        forecasts()
+        start_all(out_copies(pred, pred_out, 0))
+        scatter_plane(7), scatter_diag(9), scatter_core(11)
+        late_rows()
+        start_all(out_copies(sens, sens_out, 1))
+        scatter_z(0), scatter_z(1)
+        scatter_plane(8), scatter_diag(10)
+        scatter_z(2), scatter_z(3), scatter_z(4)
+        scatter_plane(9), scatter_diag(11)
+        scatter_plane(10)
+        scatter_z(5), scatter_z(6)
+        scatter_plane(11)
+        for j in range(7, count):
+            scatter_z(j)
+
+    gather_line(0)
+    hand_over(0, slice(0, 384)).start()
+    for m in range(1, MATS):
+        pack(m)
+        if m < 4:
+            gather_line(m)
+        hand_over(m, slice(0, hidden)).start()
     lax.fori_loop(0, count + 4, gather_step, 0)
 
-    lax.fori_loop(2, count + 8, back_step, 0)
+    lax.fori_loop(2, count, back_step, 0)
+    last_steps()
 
     grad_copy = remote(total.at[other], grad_out.at[:, core], out_send.at[2], out_recv.at[2], sibling)
     grad_copy.start()

time: 98.2 us -> 96.7 us (0.985)
  Pallas kernels: 97.2 us -> 95.7 us
    pallas_call x1, Pallas kernels: 92.9 us -> 91.3 us  [train_call(): pl.pallas_call(functools.partial(train_kernel, sizes), out_shape=(jax.Sha...]
where the time goes in v1:
time: 96.7 us; the launch traced here: 96.5 us
  Pallas kernels  95.7 us (99%)
    pallas_call x1, Pallas kernels, train_call(): pl.pallas_call(functools.partial(train_kernel, sizes), out_shape=(jax.Sha...  91.3 us
    pallas_call x1, Pallas kernels, update_call(): pl.pallas_call(functools.partial(update_kernel, sensitivity.shape[0], pre...  4.35 us

profile of v1, /device:TPU:0, one launch (start us, length us, event | category | flops | bytes accessed | tf_op | source)
XLA Modules:
  0.0 96.5 jit_solution(17366820333021253894)
XLA Ops:
  0.7 91.3 %train.1 = (f32[18,1,3072]{2,1,0:T(1,128)}, f32[126,1,3072]{2,1,0:T(1,128)}, f32[6,2,16,512]{3,2,1,0:T(8,128)}, f32[8,128]{1,0:T(8,128)}) custom-call(f32[3072,126]{1,0:T(8,128)} %seg_hbm.1, f32[18,3072]{1,0:T(8,128)} %bitcast.17, s32[24,128]{1,0:T(8,128)} %bitcast.23, f32[1,32,126]{2,1,0:T(8,128)} %bitcast.12, f32[1,5,32,512]{3,2,1,0:T(8,128)} %refs_5_.1, ...), custom_call_target="tpu_custom_call" | custom-call | flops 31406948352 | bytes 8000000 | tf_op jit(solution)/shard_map/train/pallas_call | solution.py:776
  92.0 4.4 %update.1 = (f32[18,1,3072]{2,1,0:T(1,128)}, f32[126,1,3072]{2,1,0:T(1,128)}, f32[1,32,126]{2,1,0:T(8,128)}, f32[1,5,32,512]{3,2,1,0:T(8,128)}, f32[1,32,144]{2,...) custom-call(f32[18,1,3072]{2,1,0:T(1,128)} %get-tuple-element.42.ref, ...), custom_call_target="tpu_custom_call" | custom-call | tf_op jit(solution)/shard_map/update/pallas_call | solution.py:883

commit v2 on v1

--- a/solution.py
+++ b/solution.py
@@ -396,7 +396,7 @@
         unit = t - lag
         pl.when(jnp.logical_and(unit >= 3, unit < count))(lambda: step(unit))
         if lag == 6:
-            pl.when(t == 3)(lambda: step(0))
+            pl.when(t == 4)(lambda: step(0))
 
     def gather_line(i):
         b, m = of(i)
@@ -439,19 +439,17 @@
         pl.when(jnp.logical_and(m >= 1, m <= 3))(lambda: layer_next(b, m))
         pl.when(m == 4)(backcast_step)
 
-        pl.when(i == 8)(lambda: gather_core(10))
-
         @pl.when(jnp.logical_or(i == 4, i == 8))
         def _():
             pl.when(b == 1)(lambda: feed(b))
             pl.when(b == 0)(lambda: feed_forward(b))
-            lax.fori_loop(jnp.where(b == 1, 4, 5), MATS, lambda n, carry: (theta_grad(b, n), carry)[1], 0)
-            pl.when(b == 0)(lambda: scatter_start(0))
-
-            @pl.when(b == 1)
-            def _():
-                scatter_start(1)
-                scatter_start(2)
+            def one(n, carry):
+                pl.when(jnp.logical_and(b == 1, n == 5))(lambda: gather_core(10))
+                theta_grad(b, n)
+                scatter_start(jnp.where(b == 0, 0, n - 3))
+                return carry
+
+            lax.fori_loop(jnp.where(b == 1, 4, 5), MATS, one, 0)
 
     def gather_step(t, carry):
         pl.when(t == 12)(lambda: scatter_core(0))
@@ -681,25 +679,23 @@
             arrived(11)
             theta_step(0)
 
+        @pl.when(j == count)
+        def _():
+            input_grad(0)
+            forecasts()
+            start_all(out_copies(pred, pred_out, 0))
+
+        @pl.when(j == count + 1)
+        def _():
+            late_rows()
+            start_all(out_copies(sens, sens_out, 1))
+
+        @pl.when(j >= count + 1)
+        def _():
+            scatter_z(2 * (j - count - 1))
+            scatter_z(2 * (j - count - 1) + 1)
+
         return carry
-
-    def last_steps():
-        scatter_plane(6), scatter_diag(8), scatter_core(10)
-        input_grad(0)
-        forecasts()
-        start_all(out_copies(pred, pred_out, 0))
-        scatter_plane(7), scatter_diag(9), scatter_core(11)
-        late_rows()
-        start_all(out_copies(sens, sens_out, 1))
-        scatter_z(0), scatter_z(1)
-        scatter_plane(8), scatter_diag(10)
-        scatter_z(2), scatter_z(3), scatter_z(4)
-        scatter_plane(9), scatter_diag(11)
-        scatter_plane(10)
-        scatter_z(5), scatter_z(6)
-        scatter_plane(11)
-        for j in range(7, count):
-            scatter_z(j)
 
     gather_line(0)
     hand_over(0, slice(0, 384)).start()
@@ -710,8 +706,7 @@
         hand_over(m, slice(0, hidden)).start()
     lax.fori_loop(0, count + 4, gather_step, 0)
 
-    lax.fori_loop(2, count, back_step, 0)
-    last_steps()
+    lax.fori_loop(2, count + 7, back_step, 0)
 
     grad_copy = remote(total.at[other], grad_out.at[:, core], out_send.at[2], out_recv.at[2], sibling)
     grad_copy.start()
@@ -840,8 +835,8 @@
     leaving = [
         pltpu.make_async_copy(ref, target, out_sem.at[n]) for n, (ref, target) in enumerate(zip(held[0:2] + results, targets))
     ]
-    for copy in arriving:
-        copy.start()
+    for n in (2, 3, 0, 5, 9, 13, 1, 4, 8, 12, 6, 10, 14, 7, 11, 15):
+        arriving[n].start()
     grads, norm, masters, momenta, variances = held[2], held[3], held[4:8], held[8:12], held[12:16]
     units = masters[3].shape[2]
 

time: 96.7 us -> 96.4 us (level)
  no operation moved by 1% of the time
where the time goes in v2:
time: 96.4 us; the launch traced here: 96.2 us
  Pallas kernels  95.4 us (99%)
    pallas_call x1, Pallas kernels, train_call(): pl.pallas_call(functools.partial(train_kernel, sizes), out_shape=(jax.Sha...  91 us
    pallas_call x1, Pallas kernels, update_call(): pl.pallas_call(functools.partial(update_kernel, sensitivity.shape[0], pre...  4.44 us

profile of v2, /device:TPU:0, one launch (start us, length us, event | category | flops | bytes accessed | tf_op | source)
XLA Modules:
  0.0 96.2 jit_solution(9040397700762895451)
XLA Ops:
  0.7 91.0 %train.1 = (f32[18,1,3072]{2,1,0:T(1,128)}, f32[126,1,3072]{2,1,0:T(1,128)}, f32[6,2,16,512]{3,2,1,0:T(8,128)}, f32[8,128]{1,0:T(8,128)}) custom-call(f32[3072,126]{1,0:T(8,128)} %seg_hbm.1, f32[18,3072]{1,0:T(8,128)} %bitcast.17, s32[24,128]{1,0:T(8,128)} %bitcast.23, f32[1,32,126]{2,1,0:T(8,128)} %bitcast.12, f32[1,5,32,512]{3,2,1,0:T(8,128)} %refs_5_.1, ...), custom_call_target="tpu_custom_call" | custom-call | flops 31406948352 | bytes 8000000 | tf_op jit(solution)/shard_map/train/pallas_call | solution.py:771
  91.6 4.4 %update.1 = (f32[18,1,3072]{2,1,0:T(1,128)}, f32[126,1,3072]{2,1,0:T(1,128)}, f32[1,32,126]{2,1,0:T(8,128)}, f32[1,5,32,512]{3,2,1,0:T(8,128)}, f32[1,32,144]{2,...) custom-call(f32[18,1,3072]{2,1,0:T(1,128)} %get-tuple-element.42.ref, ...), custom_call_target="tpu_custom_call" | custom-call | tf_op jit(solution)/shard_map/update/pallas_call | solution.py:878

commit v3 on v2

--- a/solution.py
+++ b/solution.py
@@ -349,8 +349,12 @@
 
     def layer_next(b, k):
         source, target = lax.rem(k + 1, 2), lax.rem(k, 2)
-        v = dot_nn(work[source], matrix(b, k)) + bias_t[pl.ds(span + k, 1), :]
-        work[target] = store_layer(b, k, slice(0, windows), v)
+
+        def body(at):
+            v = dot_nn(work[source, at, :], matrix(b, k)) + bias_t[pl.ds(span + k, 1), :]
+            work[target, at, :] = store_layer(b, k, at, v)
+
+        halves(body)
 
     def grid(value):
         return value.astype(BF).reshape(ZN, YN, XN, 2, half_rows, -1)
@@ -593,17 +597,25 @@
         work[2] = dot_nt(f_ref[...], small(b, 128)).astype(BF)
 
     def put_dz(b, k, da):
-        dz = da * slope[b, k].astype(F32)
-        work[k % 2 if isinstance(k, int) else lax.rem(k, 2)] = dz.astype(BF)
-        bias_sum[pl.ds(span + k, 1), :] = jnp.sum(add_rows(dz), axis=0, keepdims=True)
+        sums = []
+
+        def body(at):
+            dz = da(at) * slope[b, k, at, :].astype(F32)
+            work[k % 2 if isinstance(k, int) else lax.rem(k, 2), at, :] = dz.astype(BF)
+            sums.append(add_rows(dz))
+
+        halves(body)
+        bias_sum[pl.ds(span + k, 1), :] = jnp.sum(sums[0] + sums[1], axis=0, keepdims=True)
 
     def theta_step(b):
-        put_dz(b, 3, 0.5 * (dot_nt(work[0], matrix(b, 4)) + dot_nt(work[2], matrix(b, 5))))
+        put_dz(
+            b, 3, lambda at: 0.5 * (dot_nt(work[0, at, :], matrix(b, 4)) + dot_nt(work[2, at, :], matrix(b, 5)))
+        )
 
     def layer_back(b, k):
         source = lax.rem(k, 2)
         gp[b, k] = grid(dot_nn(act_t[b, k - 1], work[source]))
-        put_dz(b, k - 1, dot_nt(work[source], matrix(b, k)))
+        put_dz(b, k - 1, lambda at: dot_nt(work[source, at, :], matrix(b, k)))
 
     def theta_grad(b, m):
         gp[b, m] = grid(dot_nn(act_t[b, 3], work[jnp.where(m == 4, 0, 2)]))

time: 96.4 us -> 95.3 us (0.989)
  Pallas kernels: 95.4 us -> 94.3 us
    pallas_call x1, Pallas kernels: 91 us -> 89.9 us  [train_call(): pl.pallas_call(functools.partial(train_kernel, sizes), out_shape=(jax.Sha...]
where the time goes in v3:
time: 95.3 us; the launch traced here: 95.1 us
  Pallas kernels  94.3 us (99%)
    pallas_call x1, Pallas kernels, train_call(): pl.pallas_call(functools.partial(train_kernel, sizes), out_shape=(jax.Sha...  89.9 us
    pallas_call x1, Pallas kernels, update_call(): pl.pallas_call(functools.partial(update_kernel, sensitivity.shape[0], pre...  4.44 us

profile of v3, /device:TPU:0, one launch (start us, length us, event | category | flops | bytes accessed | tf_op | source)
XLA Modules:
  0.0 95.1 jit_solution(11161481912745454863)
XLA Ops:
  0.7 89.9 %train.1 = (f32[18,1,3072]{2,1,0:T(1,128)}, f32[126,1,3072]{2,1,0:T(1,128)}, f32[6,2,16,512]{3,2,1,0:T(8,128)}, f32[8,128]{1,0:T(8,128)}) custom-call(f32[3072,126]{1,0:T(8,128)} %seg_hbm.1, f32[18,3072]{1,0:T(8,128)} %bitcast.17, s32[24,128]{1,0:T(8,128)} %bitcast.23, f32[1,32,126]{2,1,0:T(8,128)} %bitcast.12, f32[1,5,32,512]{3,2,1,0:T(8,128)} %refs_5_.1, ...), custom_call_target="tpu_custom_call" | custom-call | flops 31406948352 | bytes 8000000 | tf_op jit(solution)/shard_map/train/pallas_call | solution.py:783
  90.5 4.4 %update.1 = (f32[18,1,3072]{2,1,0:T(1,128)}, f32[126,1,3072]{2,1,0:T(1,128)}, f32[1,32,126]{2,1,0:T(8,128)}, f32[1,5,32,512]{3,2,1,0:T(8,128)}, f32[1,32,144]{2,...) custom-call(f32[18,1,3072]{2,1,0:T(1,128)} %get-tuple-element.42.ref, ...), custom_call_target="tpu_custom_call" | custom-call | tf_op jit(solution)/shard_map/update/pallas_call | solution.py:890

commit v4 on v3

--- a/solution.py
+++ b/solution.py
@@ -192,10 +192,10 @@
     small_loads = [
         pltpu.make_async_copy(source, target, local_sem.at[4 + n])
         for n, (source, target) in enumerate(
-            [(square_hbm, square), (first_hbm, first), (head_hbm, head), (biases_hbm, biases), (ext_hbm, ext)]
+            [(first_hbm, first), (head_hbm, head), (biases_hbm, biases), (square_hbm, square), (ext_hbm, ext)]
         )
     ]
-    for load in small_loads + loads:
+    for load in small_loads:
         load.start()
 
     barrier = pltpu.get_barrier_semaphore()
@@ -218,7 +218,7 @@
         wg[core, m, z, y, x, core, :, lanes] = kept
         handed[m, :, lanes] = given
 
-    for load in small_loads:
+    for load in small_loads[:3]:
         load.wait()
     pad[...] = jnp.zeros_like(pad)
     pad[0:rows, 0:past] = first[0] * 0.5
@@ -463,9 +463,11 @@
         delayed(0, t, gather_columns)
         pl.when(t + 4 < count)(lambda: gather_line(t + 4))
 
-        @pl.when(t == 0)
-        def _():
-            for load in loads:
+        pl.when(t == 0)(lambda: start_all(loads))
+
+        @pl.when(t == 2)
+        def _():
+            for load in loads + small_loads[4:]:
                 load.wait()
             lax.fori_loop(0, tiles, prepare, 0)
             pad[...] = jnp.zeros_like(pad)
@@ -695,12 +697,14 @@
         def _():
             input_grad(0)
             forecasts()
-            start_all(out_copies(pred, pred_out, 0))
 
         @pl.when(j == count + 1)
         def _():
             late_rows()
-            start_all(out_copies(sens, sens_out, 1))
+
+        @pl.when(j == count + 5)
+        def _():
+            start_all(out_copies(sens, sens_out, 1) + out_copies(pred, pred_out, 0))
 
         @pl.when(j >= count + 1)
         def _():
@@ -711,6 +715,7 @@
 
     gather_line(0)
     hand_over(0, slice(0, 384)).start()
+    small_loads[3].wait()
     for m in range(1, MATS):
         pack(m)
         if m < 4:

time: 95.3 us -> 96 us (level)
  no operation moved by 1% of the time
where the time goes in v4:
time: 96 us; the launch traced here: 95.7 us
  Pallas kernels  94.9 us (99%)
    pallas_call x1, Pallas kernels, train_call(): pl.pallas_call(functools.partial(train_kernel, sizes), out_shape=(jax.Sha...  90.5 us
    pallas_call x1, Pallas kernels, update_call(): pl.pallas_call(functools.partial(update_kernel, sensitivity.shape[0], pre...  4.44 us

profile of v4, /device:TPU:0, one launch (start us, length us, event | category | flops | bytes accessed | tf_op | source)
XLA Modules:
  0.0 95.7 jit_solution(6170015405647373246)
XLA Ops:
  0.7 90.5 %train.1 = (f32[18,1,3072]{2,1,0:T(1,128)}, f32[126,1,3072]{2,1,0:T(1,128)}, f32[6,2,16,512]{3,2,1,0:T(8,128)}, f32[8,128]{1,0:T(8,128)}) custom-call(f32[3072,126]{1,0:T(8,128)} %seg_hbm.1, f32[18,3072]{1,0:T(8,128)} %bitcast.17, s32[24,128]{1,0:T(8,128)} %bitcast.23, f32[1,32,126]{2,1,0:T(8,128)} %bitcast.12, f32[1,5,32,512]{3,2,1,0:T(8,128)} %refs_5_.1, ...), custom_call_target="tpu_custom_call" | custom-call | flops 31406948352 | bytes 8000000 | tf_op jit(solution)/shard_map/train/pallas_call | solution.py:788
  91.1 4.4 %update.1 = (f32[18,1,3072]{2,1,0:T(1,128)}, f32[126,1,3072]{2,1,0:T(1,128)}, f32[1,32,126]{2,1,0:T(8,128)}, f32[1,5,32,512]{3,2,1,0:T(8,128)}, f32[1,32,144]{2,...) custom-call(f32[18,1,3072]{2,1,0:T(1,128)} %get-tuple-element.42.ref, ...), custom_call_target="tpu_custom_call" | custom-call | tf_op jit(solution)/shard_map/update/pallas_call | solution.py:895

commit v5 on v4

--- a/solution.py
+++ b/solution.py
@@ -395,10 +395,11 @@
         pl.when(jnp.logical_and(t >= lag, t < count + lag))(lambda: step(t - lag))
 
     def staged(lag, t, step):
-        early = t - lag + 1
+        early = t - lag + (1 if lag == 2 else 0)
         pl.when(jnp.logical_and(early >= (2 if lag == 2 else 1), early <= 2))(lambda: step(early))
-        unit = t - lag
-        pl.when(jnp.logical_and(unit >= 3, unit < count))(lambda: step(unit))
+        place = t - lag
+        formed = jnp.logical_and(jnp.logical_and(place >= 3, place <= count), place != 6)
+        pl.when(formed)(lambda: step(jnp.where(place <= 5, place, place - 1)))
         if lag == 6:
             pl.when(t == 4)(lambda: step(0))
 
@@ -656,7 +657,8 @@
     total[...] = jnp.zeros_like(total)
 
     def back_step(j, carry):
-        b, m = back_of(j)
+        unit = jnp.where(j <= 5, j, j - 1)
+        b, m = back_of(unit)
 
         staged(6, j, scatter_plane)
         staged(4, j, scatter_diag)
@@ -669,47 +671,43 @@
             theta_step(1)
             scatter_core(1)
 
-        pl.when(jnp.logical_and(m >= 1, m <= 3))(lambda: layer_back(b, m))
-
-        @pl.when(jnp.logical_or(j == 6, j == count - 1))
-        def _():
-            block = jnp.where(j == 6, 1, 0)
-            first_grads(block)
-            pl.when(j == 6)(lambda: input_grad(1))
-
-        @pl.when(j == 6)
+        layer = jnp.logical_and(m >= 1, m <= 3)
+        pl.when(jnp.logical_and(layer, j != 6))(lambda: layer_back(b, m))
+        pl.when(jnp.logical_or(j == 6, j == count))(lambda: first_grads(jnp.where(j == 6, 1, 0)))
+        pl.when(j == 6)(lambda: input_grad(1))
+
+        @pl.when(j == 7)
         def _():
             feed(0)
             theta_grad(0, 4)
 
-        @pl.when(jnp.logical_or(j == 10, j == 11))
-        def _():
-            lax.fori_loop(jnp.where(j == 10, 4, 5), MATS, lambda n, carry: (late_theta(b, n), carry)[1], 0)
-
-        pl.when(jnp.logical_and(j >= 3, j < count))(lambda: scatter_start(j))
-
-        @pl.when(j == 6)
+        @pl.when(jnp.logical_or(j == 11, j == count))
+        def _():
+            lax.fori_loop(jnp.where(j == 11, 4, 5), MATS, lambda n, carry: (late_theta(b, n), carry)[1], 0)
+
+        formed = jnp.logical_and(jnp.logical_and(j >= 3, j <= count), j != 6)
+        pl.when(formed)(lambda: scatter_start(unit))
+
+        @pl.when(j == 7)
         def _():
             arrived(11)
             theta_step(0)
 
-        @pl.when(j == count)
+        @pl.when(j == count + 1)
         def _():
             input_grad(0)
             forecasts()
 
-        @pl.when(j == count + 1)
-        def _():
-            late_rows()
-
-        @pl.when(j == count + 5)
+        pl.when(j == count + 2)(late_rows)
+
+        @pl.when(j == count + 6)
         def _():
             start_all(out_copies(sens, sens_out, 1) + out_copies(pred, pred_out, 0))
 
-        @pl.when(j >= count + 1)
-        def _():
-            scatter_z(2 * (j - count - 1))
-            scatter_z(2 * (j - count - 1) + 1)
+        @pl.when(j >= count + 2)
+        def _():
+            scatter_z(2 * (j - count - 2))
+            scatter_z(2 * (j - count - 2) + 1)
 
         return carry
 
@@ -723,7 +721,7 @@
         hand_over(m, slice(0, hidden)).start()
     lax.fori_loop(0, count + 4, gather_step, 0)
 
-    lax.fori_loop(2, count + 7, back_step, 0)
+    lax.fori_loop(2, count + 8, back_step, 0)
 
     grad_copy = remote(total.at[other], grad_out.at[:, core], out_send.at[2], out_recv.at[2], sibling)
     grad_copy.start()

time: 96 us -> 96.2 us (level)
  no operation moved by 1% of the time
where the time goes in v5:
time: 96.2 us; the launch traced here: 95.9 us
  Pallas kernels  95.1 us (99%)
    pallas_call x1, Pallas kernels, train_call(): pl.pallas_call(functools.partial(train_kernel, sizes), out_shape=(jax.Sha...  90.7 us
    pallas_call x1, Pallas kernels, update_call(): pl.pallas_call(functools.partial(update_kernel, sensitivity.shape[0], pre...  4.44 us

profile of v5, /device:TPU:0, one launch (start us, length us, event | category | flops | bytes accessed | tf_op | source)
XLA Modules:
  0.0 95.9 jit_solution(14975719980289626778)
XLA Ops:
  0.7 90.7 %train.1 = (f32[18,1,3072]{2,1,0:T(1,128)}, f32[126,1,3072]{2,1,0:T(1,128)}, f32[6,2,16,512]{3,2,1,0:T(8,128)}, f32[8,128]{1,0:T(8,128)}) custom-call(f32[3072,126]{1,0:T(8,128)} %seg_hbm.1, f32[18,3072]{1,0:T(8,128)} %bitcast.17, s32[24,128]{1,0:T(8,128)} %bitcast.23, f32[1,32,126]{2,1,0:T(8,128)} %bitcast.12, f32[1,5,32,512]{3,2,1,0:T(8,128)} %refs_5_.1, ...), custom_call_target="tpu_custom_call" | custom-call | flops 31406948352 | bytes 8000000 | tf_op jit(solution)/shard_map/train/pallas_call | solution.py:786
  91.3 4.4 %update.1 = (f32[18,1,3072]{2,1,0:T(1,128)}, f32[126,1,3072]{2,1,0:T(1,128)}, f32[1,32,126]{2,1,0:T(8,128)}, f32[1,5,32,512]{3,2,1,0:T(8,128)}, f32[1,32,144]{2,...) custom-call(f32[18,1,3072]{2,1,0:T(1,128)} %get-tuple-element.42.ref, ...), custom_call_target="tpu_custom_call" | custom-call | tf_op jit(solution)/shard_map/update/pallas_call | solution.py:893

commit v6 on v4

--- a/solution.py
+++ b/solution.py
@@ -616,11 +616,16 @@
 
     def layer_back(b, k):
         source = lax.rem(k, 2)
-        gp[b, k] = grid(dot_nn(act_t[b, k - 1], work[source]))
+        weight_grad(b, k, k - 1, source)
         put_dz(b, k - 1, lambda at: dot_nt(work[source, at, :], matrix(b, k)))
 
+    def weight_grad(b, m, layer, slot):
+        for n in range(0, hidden, 256):
+            part = slice(n, n + 256)
+            gp[b, m, :, :, :, :, :, part] = grid(dot_nn(act_t[b, layer], work[slot, :, part]))
+
     def theta_grad(b, m):
-        gp[b, m] = grid(dot_nn(act_t[b, 3], work[jnp.where(m == 4, 0, 2)]))
+        weight_grad(b, m, 3, jnp.where(m == 4, 0, 2))
 
     def first_grads(b):
         gp[b, 0, :, :, :, :, :, 0:128] = grid(dot_nn(in_t[b], work[0]).T)

time: 96 us -> 96 us (level)
  no operation moved by 1% of the time
where the time goes in v6:
time: 96 us; the launch traced here: 95.7 us
  Pallas kernels  94.9 us (99%)
    pallas_call x1, Pallas kernels, train_call(): pl.pallas_call(functools.partial(train_kernel, sizes), out_shape=(jax.Sha...  90.5 us
    pallas_call x1, Pallas kernels, update_call(): pl.pallas_call(functools.partial(update_kernel, sensitivity.shape[0], pre...  4.44 us

profile of v6, /device:TPU:0, one launch (start us, length us, event | category | flops | bytes accessed | tf_op | source)
XLA Modules:
  0.0 95.7 jit_solution(6170015405647373246)
XLA Ops:
  0.7 90.5 %train.1 = (f32[18,1,3072]{2,1,0:T(1,128)}, f32[126,1,3072]{2,1,0:T(1,128)}, f32[6,2,16,512]{3,2,1,0:T(8,128)}, f32[8,128]{1,0:T(8,128)}) custom-call(f32[3072,126]{1,0:T(8,128)} %seg_hbm.1, f32[18,3072]{1,0:T(8,128)} %bitcast.17, s32[24,128]{1,0:T(8,128)} %bitcast.23, f32[1,32,126]{2,1,0:T(8,128)} %bitcast.12, f32[1,5,32,512]{3,2,1,0:T(8,128)} %refs_5_.1, ...), custom_call_target="tpu_custom_call" | custom-call | flops 31406948352 | bytes 8000000 | tf_op jit(solution)/shard_map/train/pallas_call | solution.py:793
  91.1 4.4 %update.1 = (f32[18,1,3072]{2,1,0:T(1,128)}, f32[126,1,3072]{2,1,0:T(1,128)}, f32[1,32,126]{2,1,0:T(8,128)}, f32[1,5,32,512]{3,2,1,0:T(8,128)}, f32[1,32,144]{2,...) custom-call(f32[18,1,3072]{2,1,0:T(1,128)} %get-tuple-element.42.ref, ...), custom_call_target="tpu_custom_call" | custom-call | tf_op jit(solution)/shard_map/update/pallas_call | solution.py:900
